TPU v7x, 32 devices: a whole 2x2x4 slice. The times are simulated.
32 devices in a mesh: mem: 4 (over y, x), lat: 8 (over z, core).
Axes of the slice: x: 2, y: 2, z: 4, core: 2. Of those that a mesh axis runs over, the one named last changes fastest.
Arguments:
- cotangent: bfloat16 [4, 3, 4, 1024, 4096], P('mem', None, None, 'lat'), may hold values from -6 to 6
- legendre: bfloat16 [704, 2, 352, 512], P('lat', None, None, 'mem'), may hold values from -0.25 to 0.25
- wave_order: int32 [704], replicated, may hold values from 0 to 703, each once
- mode_depth: float32 [4], replicated, may hold values from 0.5 to 20
- diffusion: float32 [4], replicated, may hold values from 0.5 to 8
- quad_weights: float32 [512], replicated, may hold values from 0.25 to 2.5
Outputs:
- adjoint: bfloat16 [4, 3, 4, 1024, 4096], P('mem', None, None, 'lat')
Inputs may be any that keep to these rules, and one draw needn't show every extreme that they name: `wave_order`: each zonal wavenumber 0 to 703 appears exactly once; legendre's first index follows this order.
All inputs are finite; a program needn't handle non-finite values.
Results may differ from a plain program's by a relative error of at most 0.0076.
Values may be sent and summed in bfloat16 or wider, within the bound.
A program may use at most 192 MiB of HBM per device.

v0:
```python
import math

import jax
import jax.numpy as jnp
from jax import lax
from jax.sharding import PartitionSpec as P


def swapped(value, axis, distance):
    return lax.ppermute(value, axis, [(i, i ^ 1 << distance) for i in range(lax.axis_size(axis))])


def fourier_table(wave_order, lon_count):
    wave_ids = jnp.repeat(wave_order, 2)
    parity = jnp.arange(wave_ids.shape[0], dtype=jnp.int32) % 2
    longitude = jnp.arange(lon_count, dtype=jnp.int32)[:, None]
    phases = longitude * wave_ids[None, :] % lon_count
    angles = phases.astype(jnp.float32) * jnp.float32(2.0 * math.pi / lon_count)
    values = jnp.where(parity[None, :] == 0, jnp.cos(angles), -jnp.sin(angles))
    return (values.astype(jnp.bfloat16), wave_ids)


def implicit(spectral, degree, top_degree, mode_depth, diffusion):
    count_waves, half_deg, pieces, channels = spectral.shape
    levels = mode_depth.shape[0]
    values = spectral.reshape(count_waves, half_deg, pieces, 3, levels)
    degree_f = degree.astype(jnp.float32)
    scaled = (degree_f * (degree_f + 1.0) / (top_degree * (top_degree + 1.0)))[:, :, None, None]
    vorticity = values[:, :, :, 0] / (1.0 + diffusion * scaled * scaled)
    damping = 1.0 / (1.0 + mode_depth * scaled)
    divergence = damping * (values[:, :, :, 1] - mode_depth * values[:, :, :, 2])
    height = damping * (scaled * values[:, :, :, 1] + values[:, :, :, 2])
    joined = jnp.stack([vorticity, divergence, height], axis=3)
    return joined.reshape(count_waves, half_deg, pieces, channels).astype(jnp.bfloat16)


def shards(cotangent, legendre, wave_order, mode_depth, diffusion, quad_weights):
    members, fields, levels, band_rows, lon_count = cotangent.shape
    lat_count = lax.axis_size("lat")
    half_count = lat_count // 2
    half_rows = half_count * band_rows
    total_waves = wave_order.shape[0]
    count_waves = total_waves // lat_count
    half_deg = legendre.shape[2]
    channels = fields * levels
    fourier, wave_ids = fourier_table(wave_order, lon_count)
    flattened = cotangent.reshape(channels * band_rows, lon_count)
    factor = jnp.where(wave_ids == 0, 1.0, 2.0).astype(jnp.float32)
    coeffs = lax.dot_general(
        fourier, flattened, (((0,), (1,)), ((), ())), preferred_element_type=jnp.float32
    )
    coeffs = (coeffs * factor[:, None]).astype(jnp.bfloat16)
    mate_part = swapped(coeffs, "lat", lat_count.bit_length() - 2).astype(jnp.float32)
    own_part = coeffs.astype(jnp.float32)
    in_north = lax.axis_index("lat") < half_count
    outgoing = jnp.where(in_north, own_part + mate_part, mate_part - own_part).astype(jnp.bfloat16)
    received = lax.all_to_all(outgoing, "lat", split_axis=0, concat_axis=1, tiled=True)
    blocks = received.reshape(count_waves, 2, lat_count, channels, band_rows)
    even_part = blocks[:, :, :half_count]
    odd_part = blocks[:, :, half_count:]
    even_rows = jnp.transpose(even_part, (0, 1, 3, 2, 4)).reshape(
        count_waves, 2, channels, half_rows
    )
    odd_rows = jnp.transpose(odd_part, (0, 1, 3, 2, 4)).reshape(count_waves, 2, channels, half_rows)
    own_waves = lax.dynamic_slice_in_dim(
        wave_order, lax.axis_index("lat") * count_waves, count_waves
    )
    degree_base = 2 * jnp.arange(half_deg, dtype=jnp.int32)[None, :] + own_waves[:, None]
    top_degree = float(total_waves + 2 * half_deg - 2)
    piece = lax.all_gather(legendre, "mem", axis=3, tiled=True)
    even_add = jnp.einsum(
        "miy,mqcy->miqc", piece[:, 0], even_rows, preferred_element_type=jnp.float32
    )
    odd_add = jnp.einsum(
        "miy,mqcy->miqc", piece[:, 1], odd_rows, preferred_element_type=jnp.float32
    )
    spectral_even = implicit(even_add, degree_base, top_degree, mode_depth, diffusion)
    spectral_odd = implicit(odd_add, degree_base + 1, top_degree, mode_depth, diffusion)
    piece = lax.all_gather(legendre, "mem", axis=3, tiled=True)
    synth_even = jnp.einsum(
        "miy,miqc->mqcy", piece[:, 0], spectral_even, preferred_element_type=jnp.float32
    )
    synth_odd = jnp.einsum(
        "miy,miqc->mqcy", piece[:, 1], spectral_odd, preferred_element_type=jnp.float32
    )
    gridded = jnp.stack(
        [quad_weights * (synth_even + synth_odd), quad_weights * (synth_even - synth_odd)], axis=0
    ).astype(jnp.bfloat16)
    gridded = gridded.reshape(2, count_waves, 2, channels, half_count, band_rows)
    gridded = jnp.transpose(gridded, (1, 2, 0, 4, 3, 5)).reshape(
        2 * count_waves, lat_count * channels * band_rows
    )
    returned = lax.all_to_all(gridded, "lat", split_axis=1, concat_axis=0, tiled=True)
    result = lax.dot_general(
        returned, fourier, (((0,), (1,)), ((), ())), preferred_element_type=jnp.float32
    )
    result = result * jnp.float32(1.0 / lon_count)
    return result.astype(jnp.bfloat16).reshape(members, fields, levels, band_rows, lon_count)


def solution(mesh):
    placed = (P("mem", None, None, "lat", None), P("lat", None, None, "mem"), P(), P(), P(), P())
    return jax.shard_map(
        shards,
        mesh=mesh,
        in_specs=placed,
        out_specs=P("mem", None, None, "lat", None),
        check_vma=False,
    )
```

profile of v0, /device:TPU:0, one launch (start us, length us, event | category | flops | bytes accessed | tf_op | source)
XLA Modules:
  0.0 815.5 jit_solution(4151418853124231561)
XLA Ops:
  6.5 13.3 %copy.26 = bf16[88,2,352,128]{3,2,0,1:T(8,128)(2,1)} copy(bf16[88,2,352,128]{3,2,1,0:T(8,128)(2,1)} %param.7) | data formatting | bytes 31719424 | tf_op args[1]
  19.8 0.0 all-gather.2.cloned.1.call-update
  19.8 0.7 copy-done.9
  20.5 0.1 broadcast_in_dim.19
  20.6 0.2 mul.227
  20.9 92.8 %select_convert_fusion.12 = bf16[4096,1408]{1,0:T(8,128)(2,1)S(1)} fusion(s32[1408]{0:T(1024)S(1)} %mul.227, pred[1408]{0:T(1024)(128)(4,1)S(1)} %fusion.24), kind=kLoop, calls=%fused_computation.13.clone.1.clone.clone.clone.clone.clone.1 | loop fusion | flops 98041856 | bytes 11541376 | tf_op jit(solution)/shard_map/dot_general | solution.py:49
  113.7 22.5 %fusion.14 = bf16[1408,1536]{1,0:T(8,128)(2,1)} fusion(bf16[1536,4096]{1,0:T(8,128)(2,1)} %bitcast.60, f32[1408]{0:T(1024)S(1)} %compare_select_fusion, bf16[4096,1408]{1,0:T(8,128)(2,1)S(1)} %select_convert_fusion.12), kind=kOutput, calls=%fused_computation.23 | convolution fusion | flops 17721065472 | bytes 28448256 | tf_op jit(solution)/shard_map/dot_general | solution.py:49
  136.2 4.1 collective-permute-start
  140.3 186.4 %collective-permute-done = bf16[1408,1536]{1,0:T(8,128)(2,1)} collective-permute-done((bf16[1408,1536]{1,0:T(8,128)(2,1)}, bf16[1408,1536]{1,0:T(8,128)(2,1)}, u32[]{:S(2)}, u32[]{:S(2)}) %collective-permute-start) | collective-permute-done | bytes 4325408 | tf_op jit(solution)/shard_map/ppermute | solution.py:10
  326.7 7.1 fusion.13
  333.8 4.9 all-to-all-start
  338.8 0.1 dynamic_slice.3
  338.8 0.1 fusion.23
  339.0 0.0 copy-start.4
  339.0 0.0 copy-start.6
  339.0 0.6 copy-done.4
  339.6 0.1 copy-done.6
  339.7 0.0 copy-done.10
  339.7 1.3 multiply_add_fusion.1
  341.0 94.7 %all-to-all-done = bf16[8,176,1536]{2,1,0:T(8,128)(2,1)} async-done(((bf16[8,176,1536]{2,1,0:T(8,128)(2,1)}), bf16[8,176,1536]{2,1,0:T(8,128)(2,1)}, u32[]{:S(2)}, u32[]{:S(2)}) %all-to-all-start) | async-done | bytes 4325408 | tf_op jit(solution)/shard_map/all_to_all | solution.py:57
  435.7 4.6 copy.24
  440.3 2.4 slice_bitcast_fusion.10
  442.7 2.5 reshape.142
  445.2 4.0 reshape.143
  449.2 119.6 %all-gather.2.cloned.1.call-done = bf16[88,2,352,512]{3,2,0,1:T(8,128)(2,1)} async-done(((bf16[88,2,352,128]{3,2,0,1:T(8,128)(2,1)}), bf16[88,2,352,512]{3,2,0,1:T(8,128)(2,1)}) %all-gather.2.cloned.1.call-update) | async-done | bytes 63438864 | tf_op jit(solution)/shard_map/all_gather | solution.py:70
  568.8 18.1 %fusion.16 = f32[88,352,2,12]{1,3,2,0:T(8,128)} fusion(bf16[88,2,12,512]{3,2,1,0:T(8,128)(2,1)} %reshape.142, bf16[88,2,352,512]{3,2,0,1:T(8,128)(2,1)} %all-gather.2.cloned.1.call-done), kind=kOutput, calls=%fused_computation.28 | convolution fusion | flops 761266176 | bytes 37576704 | tf_op jit(solution)/shard_map/miy,mqcy->miqc/dot_general | solution.py:71
  586.9 5.7 copy.28
  592.7 25.0 %fusion.15 = f32[88,352,2,12]{1,3,2,0:T(8,128)} fusion(bf16[88,2,12,512]{3,2,1,0:T(8,128)(2,1)S(1)} %reshape.143, bf16[88,2,352,512]{3,2,0,1:T(8,128)(2,1)} %all-gather.2.cloned.1.call-done), kind=kOutput, calls=%fused_computation.27 | convolution fusion | flops 761266176 | bytes 36855808 | tf_op jit(solution)/shard_map/miy,mqcy->miqc/dot_general | solution.py:74
  617.7 4.3 copy.32
  621.9 0.0 copy-done
  621.9 0.0 copy-done.1
  622.0 0.0 copy-done.2
  622.0 0.0 copy-done.3
  622.0 0.0 copy-done.5
  622.0 0.0 copy-done.7
  622.0 1.0 multiply_convert_fusion.6
  623.0 1.9 pad_maximum_fusion
  624.9 15.4 %fusion.2 = f32[88,2,12,512]{3,2,1,0:T(8,128)} fusion(bf16[88,2,352,512]{3,2,0,1:T(8,128)(2,1)} %all-gather.2.cloned.1.call-done, bf16[88,352,2,12]{1,0,3,2:T(8,128)(2,1)S(1)} %bitcast.59), kind=kOutput, calls=%fused_computation.7 | convolution fusion | flops 761266176 | bytes 37531648 | tf_op jit(solution)/shard_map/miy,miqc->mqcy/dot_general | solution.py:83
  640.2 15.6 %multiply_convert_fusion.2 = (bf16[88,2,12,512]{3,2,1,0:T(8,128)(2,1)S(1)}, bf16[88,2,12,512]{3,2,1,0:T(8,128)(2,1)}) fusion(f32[88,2,12,512]{3,2,1,0:T(8,128)} %fusion.2, f32[512]{0:T(512)S(1)} %copy-done.8, bf16[88,2,352,512]{3,2,0,1:T(8,128)(2,1)} %all-gather.2.cloned.1.call-done, bf16[88,352,2,12]{1,0,3,2:T(8,128)(2,1)} %bitcast.58), kind=kOutput, calls=%fused_computation.25 | convolution fusion | flops 767754240 | bytes 43436032 | tf_op jit(solution)/shard_map/miy,miqc->mqcy/dot_general | solution.py:80
  655.8 5.4 reshape.145
  661.2 2.4 reshape.144
  663.6 5.5 maximum_bitcast_fusion
  669.1 3.5 copy.46
  672.6 8.8 %reshape.146 = bf16[176,8,1536]{2,0,1:T(8,128)(2,1)} reshape(bf16[88,2,2,4,12,128]{5,4,1,0,3,2:T(8,128)(2,1)} %copy.46) | data formatting | bytes 8650752 | tf_op jit(solution)/shard_map/all_to_all | solution.py:93
  681.4 4.9 all-to-all-start.1
  686.2 94.5 %select_convert_fusion.11 = bf16[4096,1408]{1,0:T(8,128)(2,1)} fusion(s32[1408]{0:T(1024)S(1)} %mul.227, pred[1408]{0:T(1024)(128)(4,1)S(1)} %fusion.24), kind=kLoop, calls=%fused_computation.13.clone.clone.1 | loop fusion | flops 98041856 | bytes 11541376 | tf_op jit(solution)/shard_map/dot_general | solution.py:94
  780.8 2.3 all-to-all-done.1
  783.1 25.3 %multiply_convert_fusion = bf16[1536,4096]{1,0:T(8,128)(2,1)} fusion(bf16[1408,1536]{1,0:T(8,128)(2,1)} %bitcast.22, bf16[4096,1408]{1,0:T(8,128)(2,1)} %select_convert_fusion.11), kind=kOutput, calls=%fused_computation.9 | convolution fusion | flops 17729323008 | bytes 28442624 | tf_op jit(solution)/shard_map/dot_general | solution.py:94
  (16 shorter events, 0.0 us)
Async XLA Ops:
  6.5 562.3 %all-gather.2.cloned.1.call-start = ((), (), s32[]{:S(2)}) async-start(), calls=%async_computation.2 | async-start | bytes 79298560 | tf_op jit(solution)/shard_map/all_gather | solution.py:70
  19.8 0.7 copy-start.9
  136.2 190.5 %collective-permute-start = (bf16[1408,1536]{1,0:T(8,128)(2,1)}, bf16[1408,1536]{1,0:T(8,128)(2,1)}, u32[]{:S(2)}, u32[]{:S(2)}) collective-permute-start(bf16[1408,1536]{1,0:T(8,128)(2,1)} %fusion.14), channel_id=1, source_target_pairs={{0,4},{1,5},{2,6},{3,7},{4,0},{5,1},{6,2},{7,3},{8,12},{9,13},{10,... | collective-permute-start | bytes 12976136 | tf_op jit(solution)/shard_map/ppermute | solution.py:10
  333.8 5.9 copy-start.10
  333.8 5.9 copy-start.11
  333.8 101.9 %all-to-all-start = ((bf16[8,176,1536]{2,1,0:T(8,128)(2,1)}), bf16[8,176,1536]{2,1,0:T(8,128)(2,1)}, u32[]{:S(2)}, u32[]{:S(2)}) async-start(bf16[8,176,1536]{2,1,0:T(8,128)(2,1)} %bitcast.54), calls=%async_computation | async-start | bytes 8650752 | tf_op jit(solution)/shard_map/all_to_all | solution.py:57
  339.0 0.7 copy-start.4
  339.0 0.7 copy-start.6
  617.6 4.3 copy-start
  617.6 4.3 copy-start.1
  617.6 4.3 copy-start.2
  617.6 4.3 copy-start.3
  617.7 4.3 copy-start.5
  617.7 4.3 copy-start.7
  624.9 15.4 %copy-start.8 = (f32[512]{0:T(512)S(1)}, f32[512]{0:T(512)}, u32[]{:S(2)}) copy-start(f32[512]{0:T(512)} %param.11) | copy-start | bytes 6148
  681.4 101.7 %all-to-all-start.1 = ((bf16[176,8,1536]{2,0,1:T(8,128)(2,1)}), bf16[176,8,1536]{2,0,1:T(8,128)(2,1)}, u32[]{:S(2)}, u32[]{:S(2)}) async-start(bf16[176,8,1536]{2,0,1:T(8,128)(2,1)} %reshape.146), calls=%async_computation.1 | async-start | bytes 8650752 | tf_op jit(solution)/shard_map/all_to_all | solution.py:93
Sparse Core Ops, SparseCore 0:
  19.9 548.8 all-gather.1
where the time goes:
time: 820 us; the launch traced here: 816 us
  waiting for transfers between devices  403 us (49%)
  other arithmetic  204 us (25%)
  matrix products  122 us (15%)
  local copies, waits for them, and re-layouts  58.7 us (7%)
  starting transfers between devices  13.9 us (2%)
  between operations  13.8 us (2%)
    ppermute x1, waiting for transfers between devices, swapped(): lax.ppermute(value, axis, [(i, i ^ 1 << distance) for i in range(lax.axis...  186 us
    all_gather x1, waiting for transfers between devices, shards(): piece = lax.all_gather(legendre, 'mem', axis=3, tiled=True)  120 us
    all_to_all x1, waiting for transfers between devices, shards(): lax.all_to_all(outgoing, 'lat', split_axis=0, concat_axis=1, tiled=True)  94.7 us
    dot_general x1, other arithmetic, shards(): lax.dot_general(returned, fourier, (((0,), (1,)), ((), ())), preferred_el...  94.5 us
    dot_general x1, other arithmetic, shards(): lax.dot_general(fourier, flattened, (((0,), (1,)), ((), ())), preferred_e...  92.8 us
    dot_general x1, matrix products, shards(): lax.dot_general(returned, fourier, (((0,), (1,)), ((), ())), preferred_el...  25.3 us
    dot_general x1, matrix products, shards(): jnp.einsum('miy,mqcy->miqc', piece[:, 1], odd_rows, preferred_element_typ...  25 us
    dot_general x1, matrix products, shards(): lax.dot_general(fourier, flattened, (((0,), (1,)), ((), ())), preferred_e...  22.5 us
  transfers between devices with their start and end apart: 4, of which 4 were waited for; matrix products, arithmetic and copies ran while one was open for 28% of the time, Pallas kernels for 0%

commit v1 on v0

v1 whole, which is shorter than its diff:
```python
import functools
import math

import jax
import jax.numpy as jnp
from jax import lax
from jax.experimental import pallas as pl
from jax.experimental.pallas import tpu as pltpu
from jax.sharding import PartitionSpec as P

CHUNKS = 2
AXES = ("lat", "mem")


def fourier_table(waves, lon_count):
    fine = 1 << ((lon_count.bit_length() - 1) // 2)
    coarse = lon_count // fine
    unit = jnp.float32(2.0 * math.pi / lon_count)
    ids = jnp.repeat(waves, 2)[None, :]
    is_cos = jnp.arange(ids.shape[1], dtype=jnp.int32)[None, :] % 2 == 0
    high = (jnp.arange(coarse, dtype=jnp.int32)[:, None] * fine * ids % lon_count).astype(jnp.float32) * unit
    low = (jnp.arange(fine, dtype=jnp.int32)[:, None] * ids % lon_count).astype(jnp.float32) * unit
    cos_high, sin_high = jnp.cos(high), jnp.sin(high)
    first = jnp.where(is_cos, cos_high, -sin_high)
    second = jnp.where(is_cos, sin_high, cos_high)
    first, second, cos_low, sin_low = lax.optimization_barrier((first, second, jnp.cos(low), jnp.sin(low)))
    values = first[:, None] * cos_low[None] - second[:, None] * sin_low[None]
    return lax.optimization_barrier(values.astype(jnp.bfloat16).reshape(lon_count, ids.shape[1]))


def spectral_kernel(
    fields, top_degree, waves_ref, coeff_ref, legendre_ref, depth_ref, diffusion_ref, weight_ref, out_ref
):
    bands, members, _, rows, width = coeff_ref.shape
    parts = legendre_ref.shape[0]
    half_deg = legendre_ref.shape[3]
    half = bands // 2
    piece = rows // fields
    group = members * piece
    wave = waves_ref[pl.program_id(0)]
    depth, diffusion, weight = depth_ref[...], diffusion_ref[...], weight_ref[...]

    def by_field(values):
        return jnp.concatenate(
            [values[e, f * piece : (f + 1) * piece] for f in range(fields) for e in range(members)], axis=0
        )

    evens, odds = [], []
    for b in range(half):
        north = coeff_ref[b, :, 0].astype(jnp.float32)
        south = coeff_ref[half + b, :, 0].astype(jnp.float32)
        evens.append(by_field(north + south).astype(jnp.bfloat16))
        odds.append(by_field(north - south).astype(jnp.bfloat16))
    synth = []
    for p, blocks in enumerate((evens, odds)):
        grid_rows = jnp.concatenate(blocks, axis=1)
        basis = jnp.concatenate([legendre_ref[s, 0, p] for s in range(parts)], axis=1)
        analysed = lax.dot_general(
            grid_rows, basis, (((1,), (1,)), ((), ())), preferred_element_type=jnp.float32
        )
        degree = 2 * lax.broadcasted_iota(jnp.int32, (1, half_deg), 1) + (wave + p)
        degree = degree.astype(jnp.float32)
        scaled = degree * (degree + 1.0) / (top_degree * (top_degree + 1.0))
        damping = 1.0 / (1.0 + depth * scaled)
        vor, div, hgt = (analysed[f * group : (f + 1) * group] for f in range(3))
        spectral = jnp.concatenate(
            [
                vor / (1.0 + diffusion * scaled * scaled),
                damping * (div - depth * hgt),
                damping * (scaled * div + hgt),
            ],
            axis=0,
        ).astype(jnp.bfloat16)
        synth.append(jnp.dot(spectral, basis, preferred_element_type=jnp.float32))
    both = (weight * (synth[0] + synth[1]), weight * (synth[0] - synth[1]))
    for side, values in enumerate(both):
        for b in range(half):
            block = values[:, b * width : (b + 1) * width]
            for e in range(members):
                out_ref[side * half + b, e, 0] = jnp.concatenate(
                    [block[f * group + e * piece : f * group + (e + 1) * piece] for f in range(fields)], axis=0
                ).astype(jnp.bfloat16)


def spectral_step(fields, top_degree, waves, coeffs, basis, depth, diffusion, weights):
    bands, members, count, rows, width = coeffs.shape
    parts, _, _, half_deg, lats = basis.shape
    whole = lambda array: pl.BlockSpec(array.shape, lambda m, waves: (0, 0))
    block = pl.BlockSpec((bands, members, 1, rows, width), lambda m, waves: (0, 0, m, 0, 0))
    flops = 8 * count * half_deg * lats * parts * members * rows
    return pl.pallas_call(
        functools.partial(spectral_kernel, fields, top_degree),
        grid_spec=pltpu.PrefetchScalarGridSpec(
            num_scalar_prefetch=1,
            grid=(count,),
            in_specs=[
                block,
                pl.BlockSpec((parts, 1, 2, half_deg, lats), lambda m, waves: (0, m, 0, 0, 0)),
                whole(depth),
                whole(diffusion),
                whole(weights),
            ],
            out_specs=block,
        ),
        out_shape=jax.ShapeDtypeStruct(coeffs.shape, jnp.bfloat16),
        compiler_params=pltpu.CompilerParams(vmem_limit_bytes=40 * 1024 * 1024),
        cost_estimate=pl.CostEstimate(
            flops=flops, bytes_accessed=2 * (basis.size + 2 * coeffs.size), transcendentals=0
        ),
    )(waves, coeffs, basis, depth, diffusion, weights)


def shards(cotangent, legendre, wave_order, mode_depth, diffusion, quad_weights):
    members, fields, levels, band_rows, lon_count = cotangent.shape
    lat_count, mem_count = lax.axis_size("lat"), lax.axis_size("mem")
    devices = lat_count * mem_count
    total_waves = wave_order.shape[0]
    lat_waves = total_waves // lat_count
    own_count = -(-lat_waves // mem_count)
    extra = own_count * mem_count - lat_waves
    half_deg = legendre.shape[2]
    channels = fields * levels
    rows = 2 * channels
    top_degree = float(total_waves + 2 * half_deg - 2)

    waves = jnp.pad(wave_order.reshape(lat_count, lat_waves), ((0, 0), (0, extra)))
    waves = waves.reshape(lat_count, mem_count, own_count)
    own_waves = waves[lax.axis_index("lat"), lax.axis_index("mem")]
    if extra:
        legendre = jnp.pad(legendre, ((0, extra), (0, 0), (0, 0), (0, 0)))
    legendre = legendre.reshape((mem_count, own_count) + legendre.shape[1:])
    step = -(-own_count // CHUNKS)
    cuts = [(lo, min(lo + step, own_count)) for lo in range(0, own_count, step)]

    flattened = cotangent.reshape(channels * band_rows, lon_count)
    depth = jnp.tile(mode_depth, mem_count * 2 * members)[:, None]
    spread = jnp.tile(diffusion, mem_count * 2 * members)[:, None]
    weights = quad_weights[None, :]

    tables, bases, received = [], [], []
    for lo, hi in cuts:
        part = legendre[:, lo:hi]
        if bases:
            part = lax.optimization_barrier((part, bases[-1]))[0]
        bases.append(lax.all_to_all(part, "mem", split_axis=0, concat_axis=0, tiled=True))
    for lo, hi in cuts:
        ids = waves[:, :, lo:hi].reshape(-1)
        table = fourier_table(ids, lon_count)
        tables.append(table)
        coeffs = lax.dot_general(
            table, flattened, (((0,), (1,)), ((), ())), preferred_element_type=jnp.float32
        )
        factor = jnp.where(jnp.repeat(ids, 2) == 0, 1.0, 2.0).astype(jnp.float32)
        coeffs = (coeffs * factor[:, None]).astype(jnp.bfloat16)
        coeffs = coeffs.reshape(devices, hi - lo, 2, fields, levels, band_rows)
        coeffs = jnp.transpose(coeffs, (0, 1, 3, 2, 4, 5)).reshape(devices, hi - lo, rows, band_rows)
        received.append(lax.all_to_all(coeffs, AXES, split_axis=0, concat_axis=0, tiled=True))
    total = None
    for (lo, hi), table, basis, coeffs in zip(cuts, tables, bases, received):
        shape = (lat_count, mem_count, hi - lo, rows, band_rows)
        gridded = spectral_step(
            fields, top_degree, own_waves[lo:hi], coeffs.reshape(shape), basis, depth, spread, weights
        )
        returned = lax.all_to_all(gridded.reshape(coeffs.shape), AXES, split_axis=0, concat_axis=0, tiled=True)
        returned = returned.reshape(devices, hi - lo, fields, 2, levels, band_rows)
        returned = jnp.transpose(returned, (0, 1, 3, 2, 4, 5)).reshape(-1, channels * band_rows)
        product = lax.dot_general(
            returned, table, (((0,), (1,)), ((), ())), preferred_element_type=jnp.float32
        )
        total = product if total is None else total + product
    result = (total * jnp.float32(1.0 / lon_count)).astype(jnp.bfloat16)
    return result.reshape(members, fields, levels, band_rows, lon_count)


def solution(mesh):
    placed = (P("mem", None, None, "lat", None), P("lat", None, None, "mem"), P(), P(), P(), P())
    return jax.shard_map(
        shards,
        mesh=mesh,
        in_specs=placed,
        out_specs=P("mem", None, None, "lat", None),
        check_vma=False,
    )
```

time: 820 us -> 462 us (0.56)
  other arithmetic: 204 us -> 8.25 us
  waiting for transfers between devices: 403 us -> 283 us
  matrix products: 122 us -> 68 us
  Pallas kernels: 0 us -> 24.1 us
  starting transfers between devices: 13.9 us -> 31 us
  between operations: 13.8 us -> 0.26 us
  local copies, waits for them, and re-layouts: 58.7 us -> 45.8 us
    dot_general x2 -> x0, other arithmetic: 187 us -> none  [the longest x1 94.5 us: shards(): lax.dot_general(returned, fourier, (((0,), (1,)), ((), ())), preferred_el...]
    ppermute x1 -> x0, waiting for transfers between devices: 186 us -> none  [swapped(): lax.ppermute(value, axis, [(i, i ^ 1 << distance) for i in range(lax.axis...]
    all_to_all x2 -> x6, waiting for transfers between devices: 97.1 us -> 283 us  [the longest x2 133 us: shards(): lax.all_to_all(part, 'mem', split_axis=0, concat_axis=0, tiled=True)]
    all_gather x1 -> x0, waiting for transfers between devices: 120 us -> none  [shards(): piece = lax.all_gather(legendre, 'mem', axis=3, tiled=True)]
    dot_general x6 -> x4, matrix products: 122 us -> 68 us  [the longest x2 38.5 us: shards(): lax.dot_general(returned, table, (((0,), (1,)), ((), ())), preferred_elem...]
    pallas_call x0 -> x2, Pallas kernels: none -> 24.1 us  [spectral_step(): pl.pallas_call(functools.partial(spectral_kernel, fields, top_degree), gr...]
    all_to_all x2 -> x6, starting transfers between devices: 9.81 us -> 31 us  [the longest x2 11.4 us: shards(): lax.all_to_all(part, 'mem', split_axis=0, concat_axis=0, tiled=True)]
    all_to_all x3 -> x2, local copies, waits for them, and re-layouts: 16.9 us -> 2.41 us  [shards(): lax.all_to_all(gridded.reshape(coeffs.shape), AXES, split_axis=0, concat_...]
  transfers between devices with their start and end apart: 4 -> 6, of which waited for: 4 -> 6; matrix products, arithmetic and copies ran while one was open for 28% -> 14% of each run, Pallas kernels for 0% -> 5%
where the time goes in v1:
time: 462 us; the launch traced here: 460 us
  waiting for transfers between devices  283 us (61%)
  matrix products  68 us (15%)
  local copies, waits for them, and re-layouts  45.8 us (10%)
  starting transfers between devices  31 us (7%)
  Pallas kernels  24.1 us (5%)
  other arithmetic  8.25 us (2%)
    all_to_all x2, waiting for transfers between devices, shards(): lax.all_to_all(part, 'mem', split_axis=0, concat_axis=0, tiled=True)  133 us
    all_to_all x2, waiting for transfers between devices, shards(): lax.all_to_all(coeffs, AXES, split_axis=0, concat_axis=0, tiled=True)  89.1 us
    all_to_all x2, waiting for transfers between devices, shards(): lax.all_to_all(gridded.reshape(coeffs.shape), AXES, split_axis=0, concat_...  60.7 us
    dot_general x2, matrix products, shards(): lax.dot_general(returned, table, (((0,), (1,)), ((), ())), preferred_elem...  38.5 us
    dot_general x2, matrix products, shards(): lax.dot_general(table, flattened, (((0,), (1,)), ((), ())), preferred_ele...  29.5 us
    pallas_call x2, Pallas kernels, spectral_step(): pl.pallas_call(functools.partial(spectral_kernel, fields, top_degree), gr...  24.1 us
    all_to_all x2, starting transfers between devices, shards(): lax.all_to_all(part, 'mem', split_axis=0, concat_axis=0, tiled=True)  11.4 us
    all_to_all x2, starting transfers between devices, shards(): lax.all_to_all(coeffs, AXES, split_axis=0, concat_axis=0, tiled=True)  11.2 us
  transfers between devices with their start and end apart: 6, of which 6 were waited for; matrix products, arithmetic and copies ran while one was open for 14% of the time, Pallas kernels for 5%

profile of v1, /device:TPU:0, one launch (start us, length us, event | category | flops | bytes accessed | tf_op | source)
XLA Modules:
  0.0 460.3 jit_solution(1613157078652929444)
XLA Ops:
  0.0 0.8 reshape.124
  0.8 0.1 fusion.33
  0.9 0.1 reshape.134
  1.0 0.1 reshape.125
  1.1 0.1 broadcast_in_dim.61
  1.2 0.1 mul.159
  1.4 0.1 broadcast_in_dim.65
  1.5 0.1 mul.174
  1.6 3.1 fusion.27
  4.8 2.6 subtract_convert_fusion
  7.3 2.7 copy-done.3
  10.0 14.7 %multiply_convert_fusion.1 = bf16[704,1536]{1,0:T(8,128)(2,1)} fusion(bf16[4096,704]{1,0:T(8,128)(2,1)S(1)} %bitcast.44, bf16[1536,4096]{1,0:T(8,128)(2,1)} %bitcast.48, f32[704]{0:T(1024)S(1)} %compare_select_fusion), kind=kOutput, calls=%fused_computation.3 | convolution fusion | flops 8860532736 | bytes 20515584 | tf_op jit(solution)/shard_map/dot_general | solution.py:150
  24.8 2.6 reshape.135
  27.3 2.1 copy.34
  29.4 7.3 %all-to-all-start.3 = ((bf16[32,11,24,128]{3,2,1,0:T(8,128)(2,1)}), bf16[32,11,24,128]{3,2,1,0:T(8,128)(2,1)S(1)}, u32[]{:S(2)}, u32[]{:S(2)}) async-start(bf16[32,11,24,128]{3,2,1,0:T(8,128)(2,1)} %bitcast.39), calls=%async_computation.3 | async-start | bytes 4325376 | tf_op jit(solution)/shard_map/all_to_all | solution.py:157
  36.7 11.1 %fusion.32 = (bf16[4,11,2,352,128]{4,3,2,1,0:T(8,128)(2,1)}, bf16[4,11,2,352,128]{4,3,2,1,0:T(8,128)(2,1)}) fusion(bf16[4,22,2,352,128]{4,3,2,1,0:T(8,128)(2,1)} %bitcast.37), kind=kLoop, calls=%fused_computation.63 | loop fusion | bytes 31719424 | tf_op jit(solution)/shard_map/slice | solution.py:142
  47.8 39.0 %all-to-all-done.3 = bf16[32,11,24,128]{3,2,1,0:T(8,128)(2,1)S(1)} async-done(((bf16[32,11,24,128]{3,2,1,0:T(8,128)(2,1)}), bf16[32,11,24,128]{3,2,1,0:T(8,128)(2,1)S(1)}, u32[]{:S(2)}, u32[]{:S(2)}) %all-to-all-start.3) | async-done | bytes 2162720 | tf_op jit(solution)/shard_map/all_to_all | solution.py:157
  86.8 5.8 %all-to-all-start.1 = ((bf16[4,11,2,352,128]{4,3,2,1,0:T(8,128)(2,1)}), bf16[4,11,2,352,128]{4,3,2,1,0:T(8,128)(2,1)}, u32[]{:S(2)}, u32[]{:S(2)}) async-start(bf16[4,11,2,352,128]{4,3,2,1,0:T(8,128)(2,1)} %get-tuple-element.24), calls=%async_computation.1 | async-start | bytes 15859712 | tf_op jit(solution)/shard_map/all_to_all | solution.py:145
  92.6 2.6 subtract_convert_fusion.1
  95.2 2.7 copy-done.4
  97.9 14.8 %multiply_convert_fusion.2 = bf16[704,1536]{1,0:T(8,128)(2,1)} fusion(bf16[4096,704]{1,0:T(8,128)(2,1)S(1)} %bitcast.46, bf16[1536,4096]{1,0:T(8,128)(2,1)} %bitcast.49, f32[704]{0:T(1024)S(1)} %compare_select_fusion.1), kind=kOutput, calls=%fused_computation.4 | convolution fusion | flops 8860532736 | bytes 20515584 | tf_op jit(solution)/shard_map/dot_general | solution.py:150
  112.7 4.0 reshape.127
  116.7 3.7 copy.29
  120.4 59.6 %all-to-all-done.1.legendre_ref = bf16[4,11,2,352,128]{4,3,2,1,0:T(8,128)(2,1)} async-done(((bf16[4,11,2,352,128]{4,3,2,1,0:T(8,128)(2,1)}), bf16[4,11,2,352,128]{4,3,2,1,0:T(8,128)(2,1)}, u32[]{:S(2)}, u32[]{:S(2)}) %all-to-all-start.1) | async-done | bytes 7929888 | tf_op jit(solution)/shard_map/all_to_all | solution.py:145
  180.0 3.9 all-to-all-start
  183.9 0.0 copy-start.5
  183.9 50.1 %all-to-all-done = bf16[32,11,24,128]{3,2,1,0:T(8,128)(2,1)} async-done(((bf16[32,11,24,128]{3,2,1,0:T(8,128)(2,1)}), bf16[32,11,24,128]{3,2,1,0:T(8,128)(2,1)}, u32[]{:S(2)}, u32[]{:S(2)}) %all-to-all-start) | async-done | bytes 2162720 | tf_op jit(solution)/shard_map/all_to_all | solution.py:157
  234.0 5.6 %all-to-all-start.4 = ((bf16[4,11,2,352,128]{4,3,2,1,0:T(8,128)(2,1)}), bf16[4,11,2,352,128]{4,3,2,1,0:T(8,128)(2,1)}, u32[]{:S(2)}, u32[]{:S(2)}) async-start(bf16[4,11,2,352,128]{4,3,2,1,0:T(8,128)(2,1)} %get-tuple-element.22), calls=%async_computation.4 | async-start | bytes 15859712 | tf_op jit(solution)/shard_map/all_to_all | solution.py:145
  239.7 0.1 broadcast_in_dim_tile.9.diffusion_ref
  239.7 0.1 broadcast_in_dim_tile.8.depth_ref
  239.8 0.1 slice_bitcast_fusion
  239.9 12.2 %shard_map.64 = bf16[8,4,11,24,128]{4,3,2,1,0:T(8,128)(2,1)S(1)} custom-call(s32[11]{0:T(128)S(1)} %get-tuple-element.40.waves_ref, bf16[8,4,11,24,128]{4,3,2,1,0:T(8,128)(2,1)} %bitcast.5.coeff_ref, bf16[4,11,2,352,128]{4,3,2,1,0:T(8,128)(2,1)} %all-to-all-done.1.legendre_ref, f32[32,1]{1,0:T(8,128)S(1)} %broadcast_in_dim_tile.8.depth_ref, ...), custom_call_target="tpu_custom_call" | custom-call | flops 1522532352 | bytes 12255232 | tf_op jit(solution)/shard_map/pallas_call | solution.py:91
  252.2 1.3 copy-done.1
  253.5 73.7 %all-to-all-done.4.legendre_ref = bf16[4,11,2,352,128]{4,3,2,1,0:T(8,128)(2,1)} async-done(((bf16[4,11,2,352,128]{4,3,2,1,0:T(8,128)(2,1)}), bf16[4,11,2,352,128]{4,3,2,1,0:T(8,128)(2,1)}, u32[]{:S(2)}, u32[]{:S(2)}) %all-to-all-start.4) | async-done | bytes 7929888 | tf_op jit(solution)/shard_map/all_to_all | solution.py:145
  327.1 3.7 all-to-all-start.2
  330.9 11.9 %shard_map.65 = bf16[8,4,11,24,128]{4,3,2,1,0:T(8,128)(2,1)S(1)} custom-call(s32[11]{0:T(128)S(1)} %get-tuple-element.39.waves_ref, bf16[8,4,11,24,128]{4,3,2,1,0:T(8,128)(2,1)S(1)} %bitcast.32, bf16[4,11,2,352,128]{4,3,2,1,0:T(8,128)(2,1)} %all-to-all-done.4.legendre_ref, f32[32,1]{1,0:T(8,128)S(1)} %broadcast_in_dim_tile.8.depth_ref, ...), custom_call_target="tpu_custom_call" | custom-call | flops 1522532352 | bytes 12255232 | tf_op jit(solution)/shard_map/pallas_call | solution.py:91
  342.8 1.3 copy-done
  344.1 36.9 %all-to-all-done.2 = bf16[32,11,24,128]{3,2,1,0:T(8,128)(2,1)} async-done(((bf16[32,11,24,128]{3,2,1,0:T(8,128)(2,1)}), bf16[32,11,24,128]{3,2,1,0:T(8,128)(2,1)}, u32[]{:S(2)}, u32[]{:S(2)}) %all-to-all-start.2) | async-done | bytes 2162720 | tf_op jit(solution)/shard_map/all_to_all | solution.py:164
  381.0 4.7 %all-to-all-start.5 = ((bf16[32,11,24,128]{3,2,1,0:T(8,128)(2,1)}), bf16[32,11,24,128]{3,2,1,0:T(8,128)(2,1)S(1)}, u32[]{:S(2)}, u32[]{:S(2)}) async-start(bf16[32,11,24,128]{3,2,1,0:T(8,128)(2,1)} %bitcast.33), calls=%async_computation.5 | async-start | bytes 4325376 | tf_op jit(solution)/shard_map/all_to_all | solution.py:164
  385.6 2.0 copy.32
  387.6 2.5 copy.33
  390.1 4.2 reshape.133
  394.3 17.4 %fusion.34 = f32[1536,4096]{1,0:T(8,128)} fusion(bf16[704,1536]{1,0:T(8,128)(2,1)} %reshape.133, bf16[4096,704]{1,0:T(8,128)(2,1)} %bitcast.47), kind=kOutput, calls=%fused_computation.65 | convolution fusion | flops 8858370048 | bytes 33095680 | tf_op jit(solution)/shard_map/dot_general | solution.py:167
  411.7 23.8 %all-to-all-done.5 = bf16[32,11,24,128]{3,2,1,0:T(8,128)(2,1)S(1)} async-done(((bf16[32,11,24,128]{3,2,1,0:T(8,128)(2,1)}), bf16[32,11,24,128]{3,2,1,0:T(8,128)(2,1)S(1)}, u32[]{:S(2)}, u32[]{:S(2)}) %all-to-all-start.5) | async-done | bytes 2162720 | tf_op jit(solution)/shard_map/all_to_all | solution.py:164
  435.5 0.4 copy.37
  435.9 1.1 copy.38
  437.0 2.3 reshape.140
  439.3 21.0 %multiply_convert_fusion = bf16[1536,4096]{1,0:T(8,128)(2,1)} fusion(f32[1536,4096]{1,0:T(8,128)} %fusion.34, bf16[704,1536]{1,0:T(8,128)(2,1)} %reshape.140, bf16[4096,704]{1,0:T(8,128)(2,1)} %bitcast.45), kind=kOutput, calls=%fused_computation | convolution fusion | flops 8877244416 | bytes 45678592 | tf_op jit(solution)/shard_map/dot_general | solution.py:167
  (16 shorter events, 0.1 us)
Async XLA Ops:
  7.3 2.7 copy-start.3
  29.4 57.4 %all-to-all-start.3 = ((bf16[32,11,24,128]{3,2,1,0:T(8,128)(2,1)}), bf16[32,11,24,128]{3,2,1,0:T(8,128)(2,1)S(1)}, u32[]{:S(2)}, u32[]{:S(2)}) async-start(bf16[32,11,24,128]{3,2,1,0:T(8,128)(2,1)} %bitcast.39), calls=%async_computation.3 | async-start | bytes 4325376 | tf_op jit(solution)/shard_map/all_to_all | solution.py:157
  86.8 93.1 %all-to-all-start.1 = ((bf16[4,11,2,352,128]{4,3,2,1,0:T(8,128)(2,1)}), bf16[4,11,2,352,128]{4,3,2,1,0:T(8,128)(2,1)}, u32[]{:S(2)}, u32[]{:S(2)}) async-start(bf16[4,11,2,352,128]{4,3,2,1,0:T(8,128)(2,1)} %get-tuple-element.24), calls=%async_computation.1 | async-start | bytes 15859712 | tf_op jit(solution)/shard_map/all_to_all | solution.py:145
  95.2 2.7 copy-start.4
  180.0 54.0 %all-to-all-start = ((bf16[32,11,24,128]{3,2,1,0:T(8,128)(2,1)}), bf16[32,11,24,128]{3,2,1,0:T(8,128)(2,1)}, u32[]{:S(2)}, u32[]{:S(2)}) async-start(bf16[32,11,24,128]{3,2,1,0:T(8,128)(2,1)} %bitcast.38), calls=%async_computation | async-start | bytes 4325376 | tf_op jit(solution)/shard_map/all_to_all | solution.py:157
  183.9 55.7 %copy-start.5 = (f32[4]{0:T(128)S(1)}, f32[4]{0:T(128)}, u32[]{:S(2)}) copy-start(f32[4]{0:T(128)} %param.10) | copy-start | bytes 52
  183.9 55.8 %copy-start.6 = (f32[4]{0:T(128)S(1)}, f32[4]{0:T(128)}, u32[]{:S(2)}) copy-start(f32[4]{0:T(128)} %param.9) | copy-start | bytes 52
  183.9 56.0 %copy-start.2 = (f32[512]{0:T(512)S(1)}, f32[512]{0:T(512)}, u32[]{:S(2)}) copy-start(f32[512]{0:T(512)} %param.11) | copy-start | bytes 6148
  234.0 93.1 %all-to-all-start.4 = ((bf16[4,11,2,352,128]{4,3,2,1,0:T(8,128)(2,1)}), bf16[4,11,2,352,128]{4,3,2,1,0:T(8,128)(2,1)}, u32[]{:S(2)}, u32[]{:S(2)}) async-start(bf16[4,11,2,352,128]{4,3,2,1,0:T(8,128)(2,1)} %get-tuple-element.22), calls=%async_computation.4 | async-start | bytes 15859712 | tf_op jit(solution)/shard_map/all_to_all | solution.py:145
  252.2 1.3 copy-start.1
  327.1 53.8 %all-to-all-start.2 = ((bf16[32,11,24,128]{3,2,1,0:T(8,128)(2,1)}), bf16[32,11,24,128]{3,2,1,0:T(8,128)(2,1)}, u32[]{:S(2)}, u32[]{:S(2)}) async-start(bf16[32,11,24,128]{3,2,1,0:T(8,128)(2,1)} %bitcast.34), calls=%async_computation.2 | async-start | bytes 4325376 | tf_op jit(solution)/shard_map/all_to_all | solution.py:164
  342.7 1.3 copy-start
  381.0 54.5 %all-to-all-start.5 = ((bf16[32,11,24,128]{3,2,1,0:T(8,128)(2,1)}), bf16[32,11,24,128]{3,2,1,0:T(8,128)(2,1)S(1)}, u32[]{:S(2)}, u32[]{:S(2)}) async-start(bf16[32,11,24,128]{3,2,1,0:T(8,128)(2,1)} %bitcast.33), calls=%async_computation.5 | async-start | bytes 4325376 | tf_op jit(solution)/shard_map/all_to_all | solution.py:164

commit v2 on v1

--- a/solution.py
+++ b/solution.py
@@ -8,7 +8,7 @@
 from jax.experimental.pallas import tpu as pltpu
 from jax.sharding import PartitionSpec as P
 
-CHUNKS = 2
+CHUNKS = 3
 AXES = ("lat", "mem")
 
 
@@ -28,16 +28,24 @@
     return lax.optimization_barrier(values.astype(jnp.bfloat16).reshape(lon_count, ids.shape[1]))
 
 
+def zero_after(array):
+    first = array[(0,) * array.ndim]
+    return (first != first).astype(jnp.int32)
+
+
 def spectral_kernel(
-    fields, top_degree, waves_ref, coeff_ref, legendre_ref, depth_ref, diffusion_ref, weight_ref, out_ref
+    fields, top_degree, scalars_ref, coeff_ref, depth_ref, diffusion_ref, weight_ref, own_ref, *refs
 ):
+    *legendre_refs, out_ref = refs
     bands, members, _, rows, width = coeff_ref.shape
-    parts = legendre_ref.shape[0]
-    half_deg = legendre_ref.shape[3]
+    half_deg, lats = own_ref.shape[3:]
+    parts = 1 + len(legendre_refs)
     half = bands // 2
     piece = rows // fields
     group = members * piece
-    wave = waves_ref[pl.program_id(0)]
+    wave = scalars_ref[1 + pl.program_id(0)]
+    per_part = lats // width
+    order = [(scalars_ref[0] ^ k) * per_part + t for k in range(parts) for t in range(per_part)]
     depth, diffusion, weight = depth_ref[...], diffusion_ref[...], weight_ref[...]
 
     def by_field(values):
@@ -46,7 +54,7 @@
         )
 
     evens, odds = [], []
-    for b in range(half):
+    for b in order:
         north = coeff_ref[b, :, 0].astype(jnp.float32)
         south = coeff_ref[half + b, :, 0].astype(jnp.float32)
         evens.append(by_field(north + south).astype(jnp.bfloat16))
@@ -54,7 +62,7 @@
     synth = []
     for p, blocks in enumerate((evens, odds)):
         grid_rows = jnp.concatenate(blocks, axis=1)
-        basis = jnp.concatenate([legendre_ref[s, 0, p] for s in range(parts)], axis=1)
+        basis = jnp.concatenate([own_ref[0, 0, p]] + [ref[0, p] for ref in legendre_refs], axis=1)
         analysed = lax.dot_general(
             grid_rows, basis, (((1,), (1,)), ((), ())), preferred_element_type=jnp.float32
         )
@@ -74,40 +82,39 @@
         synth.append(jnp.dot(spectral, basis, preferred_element_type=jnp.float32))
     both = (weight * (synth[0] + synth[1]), weight * (synth[0] - synth[1]))
     for side, values in enumerate(both):
-        for b in range(half):
-            block = values[:, b * width : (b + 1) * width]
+        for place, b in enumerate(order):
+            block = values[:, place * width : (place + 1) * width]
             for e in range(members):
                 out_ref[side * half + b, e, 0] = jnp.concatenate(
                     [block[f * group + e * piece : f * group + (e + 1) * piece] for f in range(fields)], axis=0
                 ).astype(jnp.bfloat16)
 
 
-def spectral_step(fields, top_degree, waves, coeffs, basis, depth, diffusion, weights):
+def spectral_step(fields, top_degree, start, scalars, coeffs, own, bases, depth, diffusion, weights):
     bands, members, count, rows, width = coeffs.shape
-    parts, _, _, half_deg, lats = basis.shape
-    whole = lambda array: pl.BlockSpec(array.shape, lambda m, waves: (0, 0))
-    block = pl.BlockSpec((bands, members, 1, rows, width), lambda m, waves: (0, 0, m, 0, 0))
-    flops = 8 * count * half_deg * lats * parts * members * rows
+    half_deg, lats = own.shape[3:]
+    parts = 1 + len(bases)
+    whole = lambda array: pl.BlockSpec(array.shape, lambda m, scalars: (0, 0))
+    block = pl.BlockSpec((bands, members, 1, rows, width), lambda m, scalars: (0, 0, m, 0, 0))
+    arrived = pl.BlockSpec((1, 2, half_deg, lats), lambda m, scalars: (m, 0, 0, 0))
+    held = pl.BlockSpec((1, 1, 2, half_deg, lats), lambda m, scalars: (scalars[0], start + m, 0, 0, 0))
+    basis_size = count * 2 * half_deg * lats * parts
     return pl.pallas_call(
         functools.partial(spectral_kernel, fields, top_degree),
         grid_spec=pltpu.PrefetchScalarGridSpec(
             num_scalar_prefetch=1,
             grid=(count,),
-            in_specs=[
-                block,
-                pl.BlockSpec((parts, 1, 2, half_deg, lats), lambda m, waves: (0, m, 0, 0, 0)),
-                whole(depth),
-                whole(diffusion),
-                whole(weights),
-            ],
+            in_specs=[block, whole(depth), whole(diffusion), whole(weights), held] + [arrived] * len(bases),
             out_specs=block,
         ),
         out_shape=jax.ShapeDtypeStruct(coeffs.shape, jnp.bfloat16),
         compiler_params=pltpu.CompilerParams(vmem_limit_bytes=40 * 1024 * 1024),
         cost_estimate=pl.CostEstimate(
-            flops=flops, bytes_accessed=2 * (basis.size + 2 * coeffs.size), transcendentals=0
+            flops=4 * basis_size * members * rows,
+            bytes_accessed=2 * (basis_size + 2 * coeffs.size),
+            transcendentals=0,
         ),
-    )(waves, coeffs, basis, depth, diffusion, weights)
+    )(scalars, coeffs, depth, diffusion, weights, own, *bases)
 
 
 def shards(cotangent, legendre, wave_order, mode_depth, diffusion, quad_weights):
@@ -125,7 +132,8 @@
 
     waves = jnp.pad(wave_order.reshape(lat_count, lat_waves), ((0, 0), (0, extra)))
     waves = waves.reshape(lat_count, mem_count, own_count)
-    own_waves = waves[lax.axis_index("lat"), lax.axis_index("mem")]
+    me = lax.axis_index("mem")
+    own_waves = waves[lax.axis_index("lat"), me]
     if extra:
         legendre = jnp.pad(legendre, ((0, extra), (0, 0), (0, 0), (0, 0)))
     legendre = legendre.reshape((mem_count, own_count) + legendre.shape[1:])
@@ -135,16 +143,22 @@
     flattened = cotangent.reshape(channels * band_rows, lon_count)
     depth = jnp.tile(mode_depth, mem_count * 2 * members)[:, None]
     spread = jnp.tile(diffusion, mem_count * 2 * members)[:, None]
-    weights = quad_weights[None, :]
+    weights = quad_weights.reshape(mem_count, -1)[me ^ jnp.arange(mem_count)].reshape(1, -1)
 
     tables, bases, received = [], [], []
     for lo, hi in cuts:
-        part = legendre[:, lo:hi]
-        if bases:
-            part = lax.optimization_barrier((part, bases[-1]))[0]
-        bases.append(lax.all_to_all(part, "mem", split_axis=0, concat_axis=0, tiled=True))
+        arrivals = []
+        for k in range(1, mem_count):
+            place = me ^ k
+            if len(bases) > 1:
+                place = place + zero_after(bases[-2][k - 1])
+            part = lax.dynamic_slice_in_dim(legendre, place, 1)[0, lo:hi]
+            arrivals.append(lax.ppermute(part, "mem", [(i, i ^ k) for i in range(mem_count)]))
+        bases.append(arrivals)
     for lo, hi in cuts:
         ids = waves[:, :, lo:hi].reshape(-1)
+        if tables:
+            ids = ids + zero_after(coeffs)
         table = fourier_table(ids, lon_count)
         tables.append(table)
         coeffs = lax.dot_general(
@@ -158,8 +172,9 @@
     total = None
     for (lo, hi), table, basis, coeffs in zip(cuts, tables, bases, received):
         shape = (lat_count, mem_count, hi - lo, rows, band_rows)
+        scalars = jnp.concatenate([me[None].astype(jnp.int32), own_waves[lo:hi]])
         gridded = spectral_step(
-            fields, top_degree, own_waves[lo:hi], coeffs.reshape(shape), basis, depth, spread, weights
+            fields, top_degree, lo, scalars, coeffs.reshape(shape), legendre, basis, depth, spread, weights
         )
         returned = lax.all_to_all(gridded.reshape(coeffs.shape), AXES, split_axis=0, concat_axis=0, tiled=True)
         returned = returned.reshape(devices, hi - lo, fields, 2, levels, band_rows)

time: 462 us -> 516 us (1.12)
  blocking collectives: 0 us -> 38 us
  matrix products: 68 us -> 78 us
  waiting for transfers between devices: 283 us -> 275 us
  between operations: 0.26 us -> 6.91 us
    ppermute x0 -> x9, waiting for transfers between devices: none -> 194 us  [shards(): lax.ppermute(part, 'mem', [(i, i ^ k) for i in range(mem_count)])]
    all_to_all x2 -> x0, waiting for transfers between devices: 133 us -> none  [shards(): lax.all_to_all(part, 'mem', split_axis=0, concat_axis=0, tiled=True)]
    all_to_all x2, waiting for transfers between devices: 89.1 us -> 37.4 us  [shards(): lax.all_to_all(coeffs, AXES, split_axis=0, concat_axis=0, tiled=True)]
    all_to_all x0 -> x1, blocking collectives: none -> 38 us  [shards(): lax.all_to_all(coeffs, AXES, split_axis=0, concat_axis=0, tiled=True)]
    all_to_all x2 -> x3, waiting for transfers between devices: 60.7 us -> 43.6 us  [shards(): lax.all_to_all(gridded.reshape(coeffs.shape), AXES, split_axis=0, concat_...]
    all_to_all x2 -> x0, starting transfers between devices: 11.4 us -> none  [shards(): lax.all_to_all(part, 'mem', split_axis=0, concat_axis=0, tiled=True)]
    squeeze x0 -> x2, local copies, waits for them, and re-layouts: none -> 10.6 us  [shards(): part = lax.dynamic_slice_in_dim(legendre, place, 1)[0, lo:hi]]
    ppermute x0 -> x9, starting transfers between devices: none -> 10.5 us  [shards(): lax.ppermute(part, 'mem', [(i, i ^ k) for i in range(mem_count)])]
  transfers between devices with their start and end apart: 6 -> 14, of which waited for: 6 -> 10; matrix products, arithmetic and copies ran while one was open for 14% -> 6% of each run, Pallas kernels for 5% -> 5%
where the time goes in v2:
time: 516 us; the launch traced here: 512 us
  waiting for transfers between devices  275 us (53%)
  matrix products  78 us (15%)
  local copies, waits for them, and re-layouts  50 us (10%)
  blocking collectives  38 us (7%)
  starting transfers between devices  31.1 us (6%)
  Pallas kernels  24.7 us (5%)
  other arithmetic  8.04 us (2%)
  between operations  6.91 us (1%)
    ppermute x9, waiting for transfers between devices, shards(): lax.ppermute(part, 'mem', [(i, i ^ k) for i in range(mem_count)])  194 us
    dot_general x3, matrix products, shards(): lax.dot_general(returned, table, (((0,), (1,)), ((), ())), preferred_elem...  48.8 us
    all_to_all x3, waiting for transfers between devices, shards(): lax.all_to_all(gridded.reshape(coeffs.shape), AXES, split_axis=0, concat_...  43.6 us
    all_to_all x1, blocking collectives, shards(): lax.all_to_all(coeffs, AXES, split_axis=0, concat_axis=0, tiled=True)  38 us
    all_to_all x2, waiting for transfers between devices, shards(): lax.all_to_all(coeffs, AXES, split_axis=0, concat_axis=0, tiled=True)  37.4 us
    dot_general x3, matrix products, shards(): lax.dot_general(table, flattened, (((0,), (1,)), ((), ())), preferred_ele...  29.2 us
    pallas_call x3, Pallas kernels, spectral_step(): pl.pallas_call(functools.partial(spectral_kernel, fields, top_degree), gr...  24.7 us
    all_to_all x3, starting transfers between devices, shards(): lax.all_to_all(gridded.reshape(coeffs.shape), AXES, split_axis=0, concat_...  13.8 us
  transfers between devices with their start and end apart: 14, of which 10 were waited for; matrix products, arithmetic and copies ran while one was open for 6% of the time, Pallas kernels for 5%

profile of v2, /device:TPU:0, one launch (start us, length us, event | category | flops | bytes accessed | tf_op | source)
XLA Modules:
  0.0 512.2 jit_solution(2943539936274004530)
XLA Ops:
  2.3 1.7 subtract_convert_fusion.1
  4.0 2.0 copy-done.8
  6.0 9.9 %fusion = bf16[512,1536]{1,0:T(8,128)(2,1)S(1)} fusion(bf16[4096,512]{1,0:T(8,128)(2,1)S(1)} %bitcast.102, bf16[1536,4096]{1,0:T(8,128)(2,1)} %bitcast.107, f32[512]{0:T(512)S(1)} %compare_select_fusion.3), kind=kOutput, calls=%fused_computation.8 | convolution fusion | flops 6444023808 | bytes 18352128 | tf_op jit(solution)/shard_map/dot_general | solution.py:164
  20.2 1.7 subtract_convert_fusion
  21.9 2.0 copy-done.10
  23.9 9.7 %fusion.1 = bf16[512,1536]{1,0:T(8,128)(2,1)S(1)} fusion(bf16[4096,512]{1,0:T(8,128)(2,1)S(1)} %bitcast.104, bf16[1536,4096]{1,0:T(8,128)(2,1)} %bitcast.108, f32[512]{0:T(512)S(1)} %compare_select_fusion.2), kind=kOutput, calls=%fused_computation.9 | convolution fusion | flops 6444023808 | bytes 18352128 | tf_op jit(solution)/shard_map/dot_general | solution.py:164
  33.7 1.5 reshape.233
  35.2 2.0 copy.45
  40.2 1.2 subtract_convert_fusion.2
  41.5 1.7 copy-done.4
  43.1 9.6 %fusion.2 = bf16[384,1536]{1,0:T(8,128)(2,1)} fusion(bf16[4096,384]{1,0:T(8,128)(2,1)S(1)} %bitcast.89, bf16[1536,4096]{1,0:T(8,128)(2,1)} %bitcast.109, f32[384]{0:T(512)S(1)} %compare_select_fusion.1), kind=kOutput, calls=%fused_computation.10 | convolution fusion | flops 4833017856 | bytes 16909824 | tf_op jit(solution)/shard_map/dot_general | solution.py:164
  52.7 2.5 reshape.239
  55.6 38.0 %all_to_all.30 = bf16[32,6,24,128]{3,2,1,0:T(8,128)(2,1)} all-to-all(bf16[32,6,24,128]{3,2,1,0:T(8,128)(2,1)S(1)} %bitcast.100), channel_id=1, replica_groups=mesh['mem'=4,'lat'=8] {'lat','mem'}, dimensions={0} | all-to-all | bytes 2359296 | tf_op jit(solution)/shard_map/all_to_all | solution.py:171
  93.6 2.7 all-to-all-start
  96.3 37.4 %all-to-all-done = bf16[32,8,24,128]{3,2,1,0:T(8,128)(2,1)S(1)} async-done(((bf16[32,8,24,128]{3,2,1,0:T(8,128)(2,1)}), bf16[32,8,24,128]{3,2,1,0:T(8,128)(2,1)S(1)}, u32[]{:S(2)}, u32[]{:S(2)}) %all-to-all-start) | async-done | bytes 1572896 | tf_op jit(solution)/shard_map/all_to_all | solution.py:171
  133.7 4.0 all-to-all-start.2
  137.8 7.0 %dynamic-slice_bitcast_fusion = (bf16[8,2,352,128]{3,2,1,0:T(8,128)(2,1)}, bf16[8,2,352,128]{3,2,1,0:T(8,128)(2,1)}, bf16[8,2,352,128]{3,2,1,0:T(8,128)(2,1)}, b...) fusion(bf16[4,22,2,352,128]{4,3,2,1,0:T(8,128)(2,1)} %bitcast.84, ...), kind=kLoop, calls=%fused_computation.11 | loop fusion | bytes 17301520 | tf_op jit(solution)/shard_map/squeeze | solution.py:155
  144.8 2.7 collective-permute-start.2
  148.3 43.3 %collective-permute-done.2.refs_2_ = bf16[8,2,352,128]{3,2,1,0:T(8,128)(2,1)} collective-permute-done((bf16[8,2,352,128]{3,2,1,0:T(8,128)(2,1)}, bf16[8,2,352,128]{3,2,1,0:T(8,128)(2,1)}, u32[]{:S(2)}, u32[]{:S(2)}) %collective-permute-start.2) | collective-permute-done | bytes 1441824 | tf_op jit(solution)/shard_map/ppermute | solution.py:156
  194.0 26.6 %collective-permute-done.1.refs_1_ = bf16[8,2,352,128]{3,2,1,0:T(8,128)(2,1)} collective-permute-done((bf16[8,2,352,128]{3,2,1,0:T(8,128)(2,1)}, bf16[8,2,352,128]{3,2,1,0:T(8,128)(2,1)}, u32[]{:S(2)}, u32[]{:S(2)}) %collective-permute-start.1) | collective-permute-done | bytes 1441824 | tf_op jit(solution)/shard_map/ppermute | solution.py:156
  225.5 3.7 dynamic-slice_bitcast_fusion.6
  229.5 1.6 collective-permute-start.7
  231.1 1.6 collective-permute-start.6
  233.6 23.6 %collective-permute-done.8.refs_2_ = bf16[6,2,352,128]{3,2,1,0:T(8,128)(2,1)} collective-permute-done((bf16[6,2,352,128]{3,2,1,0:T(8,128)(2,1)}, bf16[6,2,352,128]{3,2,1,0:T(8,128)(2,1)}, u32[]{:S(2)}, u32[]{:S(2)}) %collective-permute-start.8) | collective-permute-done | bytes 1081376 | tf_op jit(solution)/shard_map/ppermute | solution.py:156
  257.2 21.4 %collective-permute-done.7.refs_1_ = bf16[6,2,352,128]{3,2,1,0:T(8,128)(2,1)} collective-permute-done((bf16[6,2,352,128]{3,2,1,0:T(8,128)(2,1)}, bf16[6,2,352,128]{3,2,1,0:T(8,128)(2,1)}, u32[]{:S(2)}, u32[]{:S(2)}) %collective-permute-start.7) | collective-permute-done | bytes 1081376 | tf_op jit(solution)/shard_map/ppermute | solution.py:156
  278.6 1.3 copy-done.2
  279.8 7.3 %shard_map.66 = bf16[8,4,6,24,128]{4,3,2,1,0:T(8,128)(2,1)S(1)} custom-call(s32[7]{0:T(128)S(1)} %pad_add_fusion.2.scalars_ref, bf16[8,4,6,24,128]{4,3,2,1,0:T(8,128)(2,1)S(1)} %bitcast.79, f32[32,1]{1,0:T(8,128)S(1)} %broadcast_in_dim_tile.8.depth_ref, f32[32,1]{1,0:T(8,128)S(1)} %broadcast_in_dim_tile.9.diffusion_ref, f32[1,512]{1,0:T(1,128)S(1)} %bitcast.81, ...), custom_call_target="tpu_custom_call" | custom-call | flops 830472192 | bytes 6684672 | tf_op jit(solution)/shard_map/pallas_call | solution.py:102
  288.2 5.0 all-to-all-start.5
  293.4 9.2 %shard_map.64 = bf16[8,4,8,24,128]{4,3,2,1,0:T(8,128)(2,1)S(1)} custom-call(s32[9]{0:T(128)S(1)} %pad_add_fusion.scalars_ref, bf16[8,4,8,24,128]{4,3,2,1,0:T(8,128)(2,1)S(1)} %bitcast.76, f32[32,1]{1,0:T(8,128)S(1)} %broadcast_in_dim_tile.8.depth_ref, f32[32,1]{1,0:T(8,128)S(1)} %broadcast_in_dim_tile.9.diffusion_ref, f32[1,512]{1,0:T(1,128)S(1)} %bitcast.82, ...), custom_call_target="tpu_custom_call" | custom-call | flops 1107296256 | bytes 8912896 | tf_op jit(solution)/shard_map/pallas_call | solution.py:102
  302.6 1.5 copy.43
  304.1 18.2 %all-to-all-done.5 = bf16[32,6,24,128]{3,2,1,0:T(8,128)(2,1)} async-done(((bf16[32,6,24,128]{3,2,1,0:T(8,128)(2,1)}), bf16[32,6,24,128]{3,2,1,0:T(8,128)(2,1)}, u32[]{:S(2)}, u32[]{:S(2)}) %all-to-all-start.5) | async-done | bytes 1179680 | tf_op jit(solution)/shard_map/all_to_all | solution.py:179
  322.3 3.6 all-to-all-start.1
  325.9 2.7 collective-permute-start.5
  329.5 50.3 %collective-permute-done.5.refs_2_ = bf16[8,2,352,128]{3,2,1,0:T(8,128)(2,1)S(1)} collective-permute-done((bf16[8,2,352,128]{3,2,1,0:T(8,128)(2,1)}, bf16[8,2,352,128]{3,2,1,0:T(8,128)(2,1)S(1)}, u32[]{:S(2)}, u32[]{:S(2)}) %collective-permute-start.5) | collective-permute-done | bytes 1441824 | tf_op jit(solution)/shard_map/ppermute | solution.py:156
  379.8 27.6 %collective-permute-done.4.refs_1_ = bf16[8,2,352,128]{3,2,1,0:T(8,128)(2,1)S(1)} collective-permute-done((bf16[8,2,352,128]{3,2,1,0:T(8,128)(2,1)}, bf16[8,2,352,128]{3,2,1,0:T(8,128)(2,1)S(1)}, u32[]{:S(2)}, u32[]{:S(2)}) %collective-permute-start.4) | collective-permute-done | bytes 1441824 | tf_op jit(solution)/shard_map/ppermute | solution.py:156
  407.4 1.7 collective-permute-done.3.refs_0_
  409.1 8.3 %shard_map.65 = bf16[8,4,8,24,128]{4,3,2,1,0:T(8,128)(2,1)S(1)} custom-call(s32[9]{0:T(128)S(1)} %pad_add_fusion.1.scalars_ref, bf16[8,4,8,24,128]{4,3,2,1,0:T(8,128)(2,1)S(1)} %bitcast.75, f32[32,1]{1,0:T(8,128)S(1)} %broadcast_in_dim_tile.8.depth_ref, f32[32,1]{1,0:T(8,128)S(1)} %broadcast_in_dim_tile.9.diffusion_ref, f32[1,512]{1,0:T(1,128)S(1)} %bitcast.83, ...), custom_call_target="tpu_custom_call" | custom-call | flops 1107296256 | bytes 8912896 | tf_op jit(solution)/shard_map/pallas_call | solution.py:102
  417.4 1.5 copy.48
  418.9 5.2 %all-to-all-start.3 = ((bf16[32,8,24,128]{3,1,2,0:T(8,128)(2,1)}), bf16[32,8,24,128]{3,1,2,0:T(8,128)(2,1)S(1)}, u32[]{:S(2)}, u32[]{:S(2)}) async-start(bf16[32,8,24,128]{3,1,2,0:T(8,128)(2,1)} %copy.48), calls=%async_computation.3 | async-start | bytes 3145728 | tf_op jit(solution)/shard_map/all_to_all | solution.py:179
  424.1 1.6 copy.53
  425.6 1.6 copy.54
  427.3 3.2 reshape.244
  430.4 1.9 copy.44
  432.4 3.8 reshape.232
  436.2 25.3 %all-to-all-done.3 = bf16[32,8,24,128]{3,1,2,0:T(8,128)(2,1)S(1)} async-done(((bf16[32,8,24,128]{3,1,2,0:T(8,128)(2,1)}), bf16[32,8,24,128]{3,1,2,0:T(8,128)(2,1)S(1)}, u32[]{:S(2)}, u32[]{:S(2)}) %all-to-all-start.3) | async-done | bytes 1572896 | tf_op jit(solution)/shard_map/all_to_all | solution.py:179
  463.0 14.1 %fusion.55 = f32[1536,4096]{1,0:T(8,128)} fusion(bf16[512,1536]{1,0:T(8,128)(2,1)S(1)} %reshape.238, bf16[4096,512]{1,0:T(8,128)(2,1)} %bitcast.105), kind=kOutput, calls=%fused_computation.118 | convolution fusion | flops 6442450944 | bytes 30932992 | tf_op jit(solution)/shard_map/dot_general | solution.py:182
  477.1 11.8 %fusion.54 = f32[1536,4096]{1,0:T(8,128)} fusion(bf16[512,1536]{1,0:T(8,128)(2,1)S(1)} %copy-done.11, bf16[4096,512]{1,0:T(8,128)(2,1)S(1)} %bitcast.103), kind=kOutput, calls=%fused_computation.117 | convolution fusion | flops 6442450944 | bytes 30932992 | tf_op jit(solution)/shard_map/dot_general | solution.py:182
  488.9 22.9 %multiply_convert_fusion = bf16[1536,4096]{1,0:T(8,128)(2,1)} fusion(f32[1536,4096]{1,0:T(8,128)} %fusion.54, f32[1536,4096]{1,0:T(8,128)} %fusion.55, bf16[384,1536]{1,0:T(8,128)(2,1)} %reshape.244, bf16[4096,384]{1,0:T(8,128)(2,1)S(1)} %bitcast.90), kind=kOutput, calls=%fused_computation.1 | convolution fusion | flops 4857004032 | bytes 67239936 | tf_op jit(solution)/shard_map/dot_general | solution.py:182
  (77 shorter events, 16.6 us)
Async XLA Ops:
  0.0 232.9 %copy-start = (f32[512]{0:T(512)S(1)}, f32[512]{0:T(512)}, u32[]{:S(2)}) copy-start(f32[512]{0:T(512)} %param.11) | copy-start | bytes 6148
  4.0 2.0 copy-start.8
  16.9 16.7 %copy-start.7 = (bf16[32,8,3,2,4,128]{5,4,3,2,1,0:T(4,128)(2,1)}, bf16[32,8,3,2,4,128]{5,4,3,2,1,0:T(4,128)(2,1)S(1)}, u32[]{:S(2)}) copy-start(bf16[32,8,3,2,4,128]{5,4,3,2,1,0:T(4,128)(2,1)S(1)} %copy.40) | copy-start | bytes 4718596
  21.9 2.0 copy-start.10
  37.2 15.5 %copy-start.6 = (bf16[32,8,3,2,4,128]{5,4,3,2,1,0:T(4,128)(2,1)}, bf16[32,8,3,2,4,128]{5,4,3,2,1,0:T(4,128)(2,1)S(1)}, u32[]{:S(2)}) copy-start(bf16[32,8,3,2,4,128]{5,4,3,2,1,0:T(4,128)(2,1)S(1)} %copy.45) | copy-start | bytes 4718596
  41.4 1.7 copy-start.4
  93.6 40.1 %all-to-all-start = ((bf16[32,8,24,128]{3,2,1,0:T(8,128)(2,1)}), bf16[32,8,24,128]{3,2,1,0:T(8,128)(2,1)S(1)}, u32[]{:S(2)}, u32[]{:S(2)}) async-start(bf16[32,8,24,128]{3,2,1,0:T(8,128)(2,1)} %bitcast.94), calls=%async_computation | async-start | bytes 3145728 | tf_op jit(solution)/shard_map/all_to_all | solution.py:171
  133.7 154.4 %all-to-all-start.2 = ((bf16[32,8,24,128]{3,2,1,0:T(8,128)(2,1)}), bf16[32,8,24,128]{3,2,1,0:T(8,128)(2,1)S(1)}, u32[]{:S(2)}, u32[]{:S(2)}) async-start(bf16[32,8,24,128]{3,2,1,0:T(8,128)(2,1)} %bitcast.92), calls=%async_computation.2 | async-start | bytes 3145728 | tf_op jit(solution)/shard_map/all_to_all | solution.py:171
  144.8 46.8 %collective-permute-start.2 = (bf16[8,2,352,128]{3,2,1,0:T(8,128)(2,1)}, bf16[8,2,352,128]{3,2,1,0:T(8,128)(2,1)}, u32[]{:S(2)}, u32[]{:S(2)}) collective-permute-start(bf16[8,2,352,128]{3,2,1,0:T(8,128)(2,1)} %get-tuple-element.33), channel_id=1, source_target_pairs={{0,24},{8,16},{16,8},{24,0},{1,25},{9,17},{17,9},{25,1},{2,26},{10... | collective-permute-start | bytes 4325384 | tf_op jit(solution)/shard_map/ppermute | solution.py:156
  147.4 73.1 %collective-permute-start.1 = (bf16[8,2,352,128]{3,2,1,0:T(8,128)(2,1)}, bf16[8,2,352,128]{3,2,1,0:T(8,128)(2,1)}, u32[]{:S(2)}, u32[]{:S(2)}) collective-permute-start(bf16[8,2,352,128]{3,2,1,0:T(8,128)(2,1)} %get-tuple-element.34), channel_id=1, source_target_pairs={{0,16},{8,24},{16,0},{24,8},{1,17},{9,25},{17,1},{25,9},{2,18},{10... | collective-permute-start | bytes 4325384 | tf_op jit(solution)/shard_map/ppermute | solution.py:156
  148.0 75.0 %collective-permute-start = (bf16[8,2,352,128]{3,2,1,0:T(8,128)(2,1)}, bf16[8,2,352,128]{3,2,1,0:T(8,128)(2,1)}, u32[]{:S(2)}, u32[]{:S(2)}) collective-permute-start(bf16[8,2,352,128]{3,2,1,0:T(8,128)(2,1)} %get-tuple-element.35), channel_id=1, source_target_pairs={{0,8},{8,0},{16,24},{24,16},{1,9},{9,1},{17,25},{25,17},{2,10},{10... | collective-permute-start | bytes 4325384 | tf_op jit(solution)/shard_map/ppermute | solution.py:156
  225.5 7.2 %copy-start.12 = (f32[4]{0:T(128)S(1)}, f32[4]{0:T(128)}, u32[]{:S(2)}) copy-start(f32[4]{0:T(128)} %param.10) | copy-start | bytes 52
  225.5 7.2 %copy-start.13 = (f32[4]{0:T(128)S(1)}, f32[4]{0:T(128)}, u32[]{:S(2)}) copy-start(f32[4]{0:T(128)} %param.9) | copy-start | bytes 52
  229.2 28.0 %collective-permute-start.8 = (bf16[6,2,352,128]{3,2,1,0:T(8,128)(2,1)}, bf16[6,2,352,128]{3,2,1,0:T(8,128)(2,1)}, u32[]{:S(2)}, u32[]{:S(2)}) collective-permute-start(bf16[6,2,352,128]{3,2,1,0:T(8,128)(2,1)} %get-tuple-element.29), channel_id=1, source_target_pairs={{0,24},{8,16},{16,8},{24,0},{1,25},{9,17},{17,9},{25,1},{2,26},{10... | collective-permute-start | bytes 3244040 | tf_op jit(solution)/shard_map/ppermute | solution.py:156
  229.5 49.1 %collective-permute-start.7 = (bf16[6,2,352,128]{3,2,1,0:T(8,128)(2,1)}, bf16[6,2,352,128]{3,2,1,0:T(8,128)(2,1)}, u32[]{:S(2)}, u32[]{:S(2)}) collective-permute-start(bf16[6,2,352,128]{3,2,1,0:T(8,128)(2,1)} %get-tuple-element.30), channel_id=1, source_target_pairs={{0,16},{8,24},{16,0},{24,8},{1,17},{9,25},{17,1},{25,9},{2,18},{10... | collective-permute-start | bytes 3244040 | tf_op jit(solution)/shard_map/ppermute | solution.py:156
  231.1 47.4 %collective-permute-start.6 = (bf16[6,2,352,128]{3,2,1,0:T(8,128)(2,1)}, bf16[6,2,352,128]{3,2,1,0:T(8,128)(2,1)}, u32[]{:S(2)}, u32[]{:S(2)}) collective-permute-start(bf16[6,2,352,128]{3,2,1,0:T(8,128)(2,1)} %get-tuple-element.31), channel_id=1, source_target_pairs={{0,8},{8,0},{16,24},{24,16},{1,9},{9,1},{17,25},{25,17},{2,10},{10... | collective-permute-start | bytes 3244040 | tf_op jit(solution)/shard_map/ppermute | solution.py:156
  278.6 1.3 copy-start.2
  287.1 1.1 copy-start.3
  288.2 34.1 %all-to-all-start.5 = ((bf16[32,6,24,128]{3,2,1,0:T(8,128)(2,1)}), bf16[32,6,24,128]{3,2,1,0:T(8,128)(2,1)}, u32[]{:S(2)}, u32[]{:S(2)}) async-start(bf16[32,6,24,128]{3,2,1,0:T(8,128)(2,1)} %bitcast.80), calls=%async_computation.5 | async-start | bytes 2359296 | tf_op jit(solution)/shard_map/all_to_all | solution.py:179
  322.3 96.5 %all-to-all-start.1 = ((bf16[32,8,24,128]{3,1,2,0:T(8,128)(2,1)}), bf16[32,8,24,128]{3,1,2,0:T(8,128)(2,1)S(1)}, u32[]{:S(2)}, u32[]{:S(2)}) async-start(bf16[32,8,24,128]{3,1,2,0:T(8,128)(2,1)} %copy.43), calls=%async_computation.1 | async-start | bytes 3145728 | tf_op jit(solution)/shard_map/all_to_all | solution.py:179
  325.9 53.9 %collective-permute-start.5 = (bf16[8,2,352,128]{3,2,1,0:T(8,128)(2,1)}, bf16[8,2,352,128]{3,2,1,0:T(8,128)(2,1)S(1)}, u32[]{:S(2)}, u32[]{:S(2)}) collective-permute-start(bf16[8,2,352,128]{3,2,1,0:T(8,128)(2,1)} %get-tuple-element.32), channel_id=1, source_target_pairs={{0,24},{8,16},{16,8},{24,0},{1,25},{9,17},{17,9},{25,1},{2,26},{10... | collective-permute-start | bytes 4325384 | tf_op jit(solution)/shard_map/ppermute | solution.py:156
  328.6 78.8 %collective-permute-start.4 = (bf16[8,2,352,128]{3,2,1,0:T(8,128)(2,1)}, bf16[8,2,352,128]{3,2,1,0:T(8,128)(2,1)S(1)}, u32[]{:S(2)}, u32[]{:S(2)}) collective-permute-start(bf16[8,2,352,128]{3,2,1,0:T(8,128)(2,1)} %get-tuple-element.36), channel_id=1, source_target_pairs={{0,16},{8,24},{16,0},{24,8},{1,17},{9,25},{17,1},{25,9},{2,18},{10... | collective-permute-start | bytes 4325384 | tf_op jit(solution)/shard_map/ppermute | solution.py:156
  329.2 79.9 %collective-permute-start.3 = (bf16[8,2,352,128]{3,2,1,0:T(8,128)(2,1)}, bf16[8,2,352,128]{3,2,1,0:T(8,128)(2,1)S(1)}, u32[]{:S(2)}, u32[]{:S(2)}) collective-permute-start(bf16[8,2,352,128]{3,2,1,0:T(8,128)(2,1)} %get-tuple-element.37), channel_id=1, source_target_pairs={{0,8},{8,0},{16,24},{24,16},{1,9},{9,1},{17,25},{25,17},{2,10},{10... | collective-permute-start | bytes 4325384 | tf_op jit(solution)/shard_map/ppermute | solution.py:156
  418.9 42.7 %all-to-all-start.3 = ((bf16[32,8,24,128]{3,1,2,0:T(8,128)(2,1)}), bf16[32,8,24,128]{3,1,2,0:T(8,128)(2,1)S(1)}, u32[]{:S(2)}, u32[]{:S(2)}) async-start(bf16[32,8,24,128]{3,1,2,0:T(8,128)(2,1)} %copy.48), calls=%async_computation.3 | async-start | bytes 3145728 | tf_op jit(solution)/shard_map/all_to_all | solution.py:179
  463.0 14.2 %copy-start.9 = (bf16[64,64,512]{2,1,0:T(8,128)(2,1)S(1)}, bf16[64,64,512]{2,1,0:T(8,128)(2,1)}, u32[]{:S(2)}) copy-start(bf16[64,64,512]{2,1,0:T(8,128)(2,1)} %copy-done.8) | copy-start | bytes 12582916
  463.0 14.2 %copy-start.11 = (bf16[512,1536]{1,0:T(8,128)(2,1)S(1)}, bf16[512,1536]{1,0:T(8,128)(2,1)}, u32[]{:S(2)}) copy-start(bf16[512,1536]{1,0:T(8,128)(2,1)} %reshape.232) | copy-start | bytes 4718596
  477.1 11.8 %copy-start.5 = (bf16[64,64,384]{2,1,0:T(8,128)(2,1)S(1)}, bf16[64,64,384]{2,1,0:T(8,128)(2,1)}, u32[]{:S(2)}) copy-start(bf16[64,64,384]{2,1,0:T(8,128)(2,1)} %copy-done.4) | copy-start | bytes 9437188
  488.9 22.9 %copy-start.1 = (f32[512]{0:T(512)S(1)}, f32[512]{0:T(512)}, u32[]{:S(2)}) copy-start(f32[512]{0:T(512)} %param.11) | copy-start | bytes 6148
